TPU v7x, 256 devices: a whole 4x4x8 slice. The times are simulated.
256 devices in a mesh: grp: 4 (over y), row: 16 (over z, core), col: 4 (over x).
Axes of the slice: x: 4, y: 4, z: 8, core: 2. Of those that a mesh axis runs over, the one named last changes fastest.
Arguments:
- matrix: float32 [32768, 8192], P(('grp', 'row'), 'col'), parts along dimension 0, as said below
- basis_matrix: float32 [32768, 8192], P(('grp', 'row'), 'col'), parts along dimension 0, as said below
- panel_index: int32 [8, 2], P('grp'), parts along dimension 0, may hold values from 0 to 31, as said below
Outputs:
- projected: float32 [32768, 256], P(('grp', 'col', 'row')), parts along dimension 0
There are 4 independent parts, one for each index of `grp`. A program takes and returns all parts, laid end to end along the dimension named above; each array names one. Nothing has to cross between parts.
Inputs may be any that keep to these rules, and one draw needn't show every extreme that they name: matrix is symmetric. The columns of basis_matrix are orthonormal. `panel_index`: row h names panels of half h; some half names panel 0 and some names the last panel.
All inputs are finite; a program needn't handle non-finite values.
Results may differ from a plain program's by a relative error of at most 0.00007.
Values sent between devices are 32-bit elements; how exact they have to be, the bound alone decides.
A program may use at most 64 MiB of HBM per device.

v0:
```python
import jax
import jax.numpy as jnp
from jax import lax
from jax.sharding import PartitionSpec as P

PANEL = 128


def body(matrix, basis_matrix, panel_index):
    cols_here = matrix.shape[1]
    col_count = lax.axis_size("col")
    half_order = cols_here * col_count // 2
    col_place = lax.axis_index("col")
    panel_slots = panel_index.shape[1]
    panel_width = panel_slots * PANEL
    masked_parts = []
    for which_half in range(2):
        for panel_slot in range(panel_slots):
            global_start = which_half * half_order + panel_index[which_half, panel_slot] * PANEL
            owner_col = global_start // cols_here
            local_start = jnp.clip(global_start - owner_col * cols_here, 0, cols_here - PANEL)
            column_piece = lax.dynamic_slice_in_dim(basis_matrix, local_start, PANEL, 1)
            masked_parts.append(
                jnp.where(owner_col == col_place, column_piece, jnp.zeros_like(column_piece))
            )
    masked = jnp.concatenate(masked_parts, axis=1)
    columns = lax.psum(masked, "col")
    gathered = lax.all_gather(columns, "row", axis=0, tiled=True)
    needed = lax.dynamic_slice_in_dim(gathered, col_place * cols_here, cols_here, 0)
    partial_value = jnp.dot(
        matrix, needed, precision=lax.Precision.HIGHEST, preferred_element_type=jnp.float32
    )
    summed = lax.psum(partial_value, "col")
    images = lax.dynamic_slice_in_dim(
        summed, col_place // (col_count // 2) * panel_width, panel_width, 1
    )
    contribution = lax.dot_general(
        basis_matrix,
        images,
        (((0,), (0,)), ((), ())),
        precision=lax.Precision.HIGHEST,
        preferred_element_type=jnp.float32,
    )
    return lax.psum_scatter(contribution, "row", scatter_dimension=0, tiled=True)


def solution(mesh):
    return jax.shard_map(
        body,
        mesh=mesh,
        in_specs=(P(("grp", "row"), "col"), P(("grp", "row"), "col"), P("grp", None)),
        out_specs=P(("grp", "col", "row"), None),
        check_vma=False,
    )
```

profile of v0, /device:TPU:16, one launch (start us, length us, event | category | flops | bytes accessed | tf_op | source)
XLA Modules:
  0.0 307.7 jit_solution(359407171462942444)
XLA Ops:
  6.5 0.0 all-reduce.3.cloned.1.call-start
  6.5 1.4 fusion.8
  10.5 1.9 dynamic-slice_select_fusion.3
  12.4 1.0 pad_maximum_fusion
  13.5 0.0 all-reduce.3.cloned.1.call-update
  13.5 0.0 all-gather.2.cloned.1.call-start
  13.6 53.8 %all-reduce.3.cloned.1.call-done = f32[512,512]{1,0:T(8,128)} async-done(((f32[512,512]{1,0:T(8,128)}), f32[512,512]{1,0:T(8,128)}) %all-reduce.3.cloned.1.call-update) | async-done | bytes 1048592 | tf_op jit(solution)/shard_map/psum | solution.py:27
  67.3 0.0 all-gather.2.cloned.1.call-update
  67.4 0.0 all-reduce.5.cloned.1.call-start
  67.4 98.2 %all-gather.2.cloned.1.call-done = f32[8192,512]{1,0:T(8,128)} async-done(((f32[512,512]{1,0:T(8,128)}), f32[8192,512]{1,0:T(8,128)}) %all-gather.2.cloned.1.call-update) | async-done | bytes 16777232 | tf_op jit(solution)/shard_map/all_gather | solution.py:28
  165.6 16.6 %fusion.2 = f32[512,512]{0,1:T(8,128)} fusion(f32[512,2048]{1,0:T(8,128)} %param.3, f32[8192,512]{1,0:T(8,128)} %all-gather.2.cloned.1.call-done, s32[]{:T(128)S(6)} %select_n.65), kind=kOutput, calls=%fused_computation.3 | convolution fusion | flops 6442450944 | bytes 9437188 | tf_op jit(solution)/shard_map/dot_general | solution.py:30
  182.3 0.0 all-reduce.5.cloned.1.call-update
  182.3 0.0 reduce-scatter.2.cloned.1.call-start
  182.4 49.5 %all-reduce.5.cloned.1.call-done = f32[512,512]{0,1:T(8,128)} async-done(((f32[512,512]{0,1:T(8,128)}), f32[512,512]{0,1:T(8,128)}) %all-reduce.5.cloned.1.call-update) | async-done | bytes 1048592 | tf_op jit(solution)/shard_map/psum | solution.py:33
  231.9 7.3 %convolution_bitcast_fusion = f32[2048,256]{0,1:T(8,128)} fusion(f32[512,2048]{1,0:T(8,128)} %param.4, f32[512,512]{0,1:T(8,128)} %all-reduce.5.cloned.1.call-done, s32[]{:T(128)S(6)} %select_n.67), kind=kOutput, calls=%fused_computation.2 | convolution fusion | flops 3221225472 | bytes 6815748 | tf_op jit(solution)/shard_map/dot_general | solution.py:37
  239.2 0.0 reduce-scatter.2.cloned.1.call-update
  239.2 60.2 %reduce-scatter.2.cloned.1.call-done = f32[128,256]{0,1:T(8,128)} async-done(((f32[2048,256]{0,1:T(8,128)}), f32[128,256]{0,1:T(8,128)}) %reduce-scatter.2.cloned.1.call-update) | async-done | bytes 131088 | tf_op jit(solution)/shard_map/reduce_scatter | solution.py:44
  299.5 1.7 copy.4
Async XLA Ops:
  6.5 60.8 %all-reduce.3.cloned.1.call-start = ((), (), s32[]{:S(2)}) async-start(), calls=%async_computation.1 | async-start | bytes 2097152 | tf_op jit(solution)/shard_map/psum | solution.py:27
  13.5 152.1 %all-gather.2.cloned.1.call-start = ((), (), s32[]{:S(2)}) async-start(), calls=%async_computation.2 | async-start | bytes 17825792 | tf_op jit(solution)/shard_map/all_gather | solution.py:28
  67.4 164.5 %all-reduce.5.cloned.1.call-start = ((), (), s32[]{:S(2)}) async-start(), calls=%async_computation.3 | async-start | bytes 2097152 | tf_op jit(solution)/shard_map/psum | solution.py:33
  182.3 117.2 %reduce-scatter.2.cloned.1.call-start = ((), (), s32[]{:S(2)}) async-start(), calls=%async_computation.4 | async-start | bytes 2228224 | tf_op jit(solution)/shard_map/reduce_scatter | solution.py:44
Sparse Core Ops, SparseCore 0:
  13.6 53.6 all-reduce.2
  69.3 96.2 all-gather.1
  182.4 49.4 all-reduce.4
  239.4 60.0 reduce-scatter.1
where the time goes:
time: 308 us
  waiting for transfers between devices  262 us (85%)
  matrix products  24 us (8%)
  between operations  15.7 us (5%)
  local copies, waits for them, and re-layouts  3.08 us (1%)
    all_gather x1, waiting for transfers between devices, body(): gathered = lax.all_gather(columns, 'row', axis=0, tiled=True)  98.2 us
    reduce_scatter x1, waiting for transfers between devices, body(): lax.psum_scatter(contribution, 'row', scatter_dimension=0, tiled=True)  60.2 us
    psum x1, waiting for transfers between devices, body(): columns = lax.psum(masked, 'col')  53.8 us
    psum x1, waiting for transfers between devices, body(): summed = lax.psum(partial_value, 'col')  49.5 us
    dot_general x1, matrix products, body(): jnp.dot(matrix, needed, precision=lax.Precision.HIGHEST, preferred_elemen...  16.6 us
    dot_general x1, matrix products, body(): lax.dot_general(basis_matrix, images, (((0,), (0,)), ((), ())), precision...  7.33 us
  transfers between devices with their start and end apart: 4, of which 4 were waited for; matrix products, arithmetic and copies ran while one was open for 0% of the time, Pallas kernels for 0%

commit v1 on v0

v1 whole, which is shorter than its diff:
```python
import functools

import jax
import jax.numpy as jnp
from jax import lax
from jax.experimental import pallas as pl
from jax.experimental.pallas import tpu as pltpu
from jax.sharding import PartitionSpec as P

PANEL = 128
MESH = pl.DeviceIdType.MESH
PLANES = 8
COLS = 4
UNITS = 2
BF16 = jnp.bfloat16
F32 = jnp.float32


def split(value):
    high = value.astype(BF16)
    return high, (value - high.astype(F32)).astype(BF16)


def dot3(a_high, a_low, b_high, b_low):
    total = jnp.dot(a_high, b_high, preferred_element_type=F32)
    total += jnp.dot(a_high, b_low, preferred_element_type=F32)
    total += jnp.dot(a_low, b_high, preferred_element_type=F32)
    return total


def kernel(
    index_ref, matrix_hbm, basis_hbm, out_ref,
    matrix_v, basis_v, m_high, m_low, qt_high, qt_low,
    pair_out, pair_in, ring, chosen, x_high, x_low,
    image, image_in, image_sum, image_pair,
    proj, proj_in, proj_sum, up_out, up_in, down_out, down_in,
    load_sem, pair_s, pair_r, up_s, up_r, down_s, down_r,
    cross_s, cross_r, twin_s, twin_r, swap_s, swap_r, half_s, half_r,
    mate_s, mate_r, sum_up_s, sum_up_r, sum_down_s, sum_down_r,
):
    grp = lax.axis_index("grp")
    row = lax.axis_index("row")
    col = lax.axis_index("col")
    plane = row // 2
    core = lax.rem(row, 2)
    half = col // 2
    slot = lax.rem(col, 2)
    rows = basis_v.shape[0]
    cols = basis_v.shape[1]
    unit = rows // UNITS
    piece = cols // (2 * PLANES)
    per_col = cols // PANEL

    def at(r, c):
        return (grp, r, c)

    twin = at(row + 1 - 2 * core, col)
    above = at(lax.rem(plane + 1, PLANES) * 2 + core, col)
    below = at(lax.rem(plane + PLANES - 1, PLANES) * 2 + core, col)
    pair = at(row, col + 1 - 2 * slot)
    mirror = at(row, 3 - col)
    across = at(row, lax.rem(col + 2, COLS))

    load_basis = pltpu.make_async_copy(basis_hbm, basis_v, load_sem.at[0])
    load_matrix = pltpu.make_async_copy(matrix_hbm, matrix_v, load_sem.at[1])
    load_basis.start()
    load_matrix.start()

    barrier = pltpu.get_barrier_semaphore()
    for other in (twin, above, below, pair, mirror, across):
        pl.semaphore_signal(barrier, inc=1, device_id=other, device_id_type=MESH)
    pl.semaphore_wait(barrier, 6)

    sends = []

    def send(src, dst, send_sem, recv_sem, target):
        copy = pltpu.make_async_remote_copy(
            src_ref=src, dst_ref=dst, send_sem=send_sem, recv_sem=recv_sem,
            device_id=target, device_id_type=MESH,
        )
        copy.start()
        sends.append(copy)

    def arrived(ref, sem):
        pltpu.make_async_copy(ref, ref, sem).wait()

    def part(u):
        return pl.ds(u * unit, unit)

    load_basis.wait()

    own = index_ref[half, slot] - slot * per_col
    other = index_ref[half, 1 - slot] - slot * per_col
    span_rows = min(64, rows)

    def pick(i, carry):
        at_rows = pl.ds(pl.multiple_of(i * span_rows, span_rows), span_rows)
        own_v = jnp.full((span_rows, PANEL), own, jnp.int32)
        other_v = jnp.full((span_rows, PANEL), other, jnp.int32)
        own_value = jnp.zeros((span_rows, PANEL), F32)
        other_value = own_value
        for j in range(per_col):
            value = basis_v[at_rows, j * PANEL:(j + 1) * PANEL]
            own_value = jnp.where(own_v == j, value, own_value)
            other_value = jnp.where(other_v == j, value, other_value)
        ring[0, at_rows] = own_value
        pair_out[at_rows] = other_value
        return carry

    lax.fori_loop(0, rows // span_rows, pick, 0)
    for u in range(UNITS):
        send(pair_out.at[part(u)], pair_in.at[part(u)], pair_s.at[u], pair_r.at[u], pair)

    def split_matrix(b):
        at_cols = pl.ds(b * rows, rows)
        high, low = split(matrix_v[:, at_cols])
        m_high[:, at_cols] = high
        m_low[:, at_cols] = low

    def split_basis(b):
        def body(i, carry):
            at_cols = pl.ds(pl.multiple_of(b * rows + i * PANEL, PANEL), PANEL)
            high, low = split(basis_v[:, at_cols].T)
            qt_high[at_cols, :] = high
            qt_low[at_cols, :] = low
            return carry
        lax.fori_loop(0, rows // PANEL, body, 0)

    cross = []

    def deliver(d, u):
        source = lax.rem(plane + PLANES - d, PLANES)
        target = source // 2
        odd = lax.rem(source, 2)
        src = ring.at[d, part(u)]
        dst = chosen.at[2 * odd + core, col, part(u)]
        sem = cross_r.at[odd, col, u]
        copy = pltpu.make_async_remote_copy(
            src_ref=src, dst_ref=dst, send_sem=cross_s.at[d, u], recv_sem=sem,
            device_id=at(row, target), device_id_type=MESH,
        )

        @pl.when(target != col)
        def _():
            copy.start()

        @pl.when(target == col)
        def _():
            pltpu.make_async_copy(src, dst, sem).start()

        cross.append((target, copy))

    def go_up(d, u):
        send(ring.at[d, part(u)], ring.at[d + 1, part(u)], up_s.at[d, u], up_r.at[d, u], above)

    def go_down(d, u):
        send(
            ring.at[(PLANES - d) % PLANES, part(u)], ring.at[PLANES - 1 - d, part(u)],
            down_s.at[d, u], down_r.at[d, u], below,
        )

    for u in range(UNITS):
        arrived(pair_in.at[part(u)], pair_r.at[u])
        ring[0, part(u)] = ring[0, part(u)] + pair_in[part(u)]
        go_up(0, u)
        go_down(0, u)
        deliver(0, u)
    load_matrix.wait()
    work = [functools.partial(split_matrix, b) for b in range(4)]
    work += [functools.partial(split_basis, b) for b in range(4)]
    for d in range(1, 5):
        for u in range(UNITS):
            if work:
                work.pop(0)()
            if d < 4 or u == 0:
                arrived(ring.at[d, part(u)], up_r.at[d - 1, u])
                if d < 3 or (d == 3 and u == 0):
                    go_up(d, u)
            if d < 4 or u == 1:
                arrived(ring.at[PLANES - d, part(u)], down_r.at[d - 1, u])
                if d < 3 or (d == 3 and u == 1):
                    go_down(d, u)
            deliver(d, u)
            if d < 4:
                deliver(PLANES - d, u)

    def prepare(block):
        for h in range(2):
            value = jnp.concatenate([chosen[block, 2 * h], chosen[block, 2 * h + 1]], axis=1)
            x_high[h], x_low[h] = split(value)

    step = 256 if rows % 256 == 0 else rows

    def multiply(block, h, first):
        at_cols = pl.ds(pl.multiple_of(block * rows, rows), rows)

        def body(i, carry):
            at_rows = pl.ds(pl.multiple_of(i * step, step), step)
            value = dot3(m_high[at_rows, at_cols], m_low[at_rows, at_cols], x_high[h], x_low[h])
            for q in range(2):
                term = value[:, q * PANEL:(q + 1) * PANEL]
                image[2 * h + q, at_rows] = term if first else image[2 * h + q, at_rows] + term
            return carry
        lax.fori_loop(0, rows // step, body, 0)

    for odd in range(2):
        for p in range(COLS):
            for u in range(UNITS):
                ref = chosen.at[2 * odd + core, p, part(u)]
                arrived(ref, cross_r.at[odd, p, u])
                send(ref, ref, twin_s.at[odd, p, u], twin_r.at[odd, p, u], twin)
        prepare(2 * odd + core)
        multiply(2 * odd + core, 0, odd == 0)
        multiply(2 * odd + core, 1, odd == 0)
    for odd in range(2):
        for p in range(COLS):
            for u in range(UNITS):
                arrived(chosen.at[2 * odd + 1 - core, p, part(u)], twin_r.at[odd, p, u])
        prepare(2 * odd + 1 - core)
        multiply(2 * odd + 1 - core, 1 - half, False)
        if odd == 1:
            for q in range(2):
                for u in range(UNITS):
                    send(
                        image.at[2 * (1 - half) + q, part(u)], image_in.at[q, part(u)],
                        swap_s.at[q, u], swap_r.at[q, u], mirror,
                    )
        multiply(2 * odd + 1 - core, half, False)

    for q in range(2):
        for u in range(UNITS):
            arrived(image_in.at[q, part(u)], swap_r.at[q, u])
            image_sum[q, part(u)] = image[2 * half + q, part(u)] + image_in[q, part(u)]
            send(
                image_sum.at[q, part(u)], image_pair.at[q, part(u)],
                half_s.at[q, u], half_r.at[q, u], pair,
            )

    def project(q, parity):
        def body(i, carry):
            at_rows = pl.ds(pl.multiple_of((2 * i + parity) * piece, piece), piece)
            proj[q, parity, i] = dot3(
                qt_high[at_rows, :], qt_low[at_rows, :],
                x_high[q, :, :PANEL], x_low[q, :, :PANEL],
            )
            return carry
        lax.fori_loop(0, PLANES, body, 0)

    near = piece // 2

    def span(d, up):
        if d < 4:
            return pl.ds(0, piece)
        return pl.ds(0, near) if up else pl.ds(near, near)

    def sum_step(q, d):
        for up in (True, False):
            buf_out, buf_in = (up_out, up_in) if up else (down_out, down_in)
            s_sem, r_sem = (sum_up_s, sum_up_r) if up else (sum_down_s, sum_down_r)
            target = lax.rem(plane + (d if up else PLANES - d), PLANES)
            here = span(d, up)
            if d < 4:
                got = span(d + 1, up)
                arrived(buf_in.at[q, d, got], r_sem.at[q, d])
                buf_out[q, d, here] = proj_sum[q, target]
                buf_out[q, d, got] = buf_out[q, d, got] + buf_in[q, d, got]
            else:
                buf_out[q, d, here] = proj_sum[q, target, here]
            send(
                buf_out.at[q, d, here], buf_in.at[q, d - 1, here],
                s_sem.at[q, d], r_sem.at[q, d - 1], above if up else below,
            )

    def begin(q):
        for u in range(UNITS):
            arrived(image_pair.at[q, part(u)], half_r.at[q, u])
        high, low = split(image_sum[q] + image_pair[q])
        x_high[q, :, :PANEL] = high
        x_low[q, :, :PANEL] = low
        project(q, 1 - core)
        send(proj.at[q, 1 - core], proj_in.at[q], mate_s.at[q], mate_r.at[q], twin)
        project(q, core)

    def combine(q):
        arrived(proj_in.at[q], mate_r.at[q])
        proj_sum[q] = proj[q, core] + proj_in[q]

    def finish(q):
        arrived(up_in.at[q, 0], sum_up_r.at[q, 0])
        arrived(down_in.at[q, 0], sum_down_r.at[q, 0])
        out_ref[:, q * PANEL:(q + 1) * PANEL] = proj_sum[q, plane] + up_in[q, 0] + down_in[q, 0]

    begin(0)
    combine(0)
    sum_step(0, 4)
    begin(1)
    sum_step(0, 3)
    combine(1)
    sum_step(1, 4)
    sum_step(0, 2)
    sum_step(1, 3)
    sum_step(0, 1)
    sum_step(1, 2)
    finish(0)
    sum_step(1, 1)
    finish(1)

    for copy in sends:
        copy.wait_send()
    for target, copy in cross:
        @pl.when(target != col)
        def _(copy=copy):
            copy.wait_send()


def body(matrix, basis_matrix, panel_index):
    rows, cols = matrix.shape
    piece = cols // (2 * PLANES)
    vmem = pltpu.VMEM
    dma = pltpu.SemaphoreType.DMA
    return pl.pallas_call(
        kernel,
        out_shape=jax.ShapeDtypeStruct((piece, 2 * PANEL), F32),
        in_specs=[
            pl.BlockSpec(memory_space=pltpu.SMEM),
            pl.BlockSpec(memory_space=pl.ANY),
            pl.BlockSpec(memory_space=pl.ANY),
        ],
        out_specs=pl.BlockSpec(memory_space=pltpu.VMEM),
        scratch_shapes=[
            vmem((rows, cols), F32),
            vmem((rows, cols), F32),
            vmem((rows, cols), BF16),
            vmem((rows, cols), BF16),
            vmem((cols, rows), BF16),
            vmem((cols, rows), BF16),
            vmem((rows, PANEL), F32),
            vmem((rows, PANEL), F32),
            vmem((PLANES, rows, PANEL), F32),
            vmem((4, COLS, rows, PANEL), F32),
            vmem((2, rows, 2 * PANEL), BF16),
            vmem((2, rows, 2 * PANEL), BF16),
            vmem((4, rows, PANEL), F32),
            vmem((2, rows, PANEL), F32),
            vmem((2, rows, PANEL), F32),
            vmem((2, rows, PANEL), F32),
            vmem((2, 2, PLANES, piece, PANEL), F32),
            vmem((2, PLANES, piece, PANEL), F32),
            vmem((2, PLANES, piece, PANEL), F32),
            vmem((2, 5, piece, PANEL), F32),
            vmem((2, 4, piece, PANEL), F32),
            vmem((2, 5, piece, PANEL), F32),
            vmem((2, 4, piece, PANEL), F32),
            dma((2,)),
            dma((UNITS,)), dma((UNITS,)),
            dma((4, UNITS)), dma((4, UNITS)),
            dma((4, UNITS)), dma((4, UNITS)),
            dma((PLANES, UNITS)), dma((2, COLS, UNITS)),
            dma((2, COLS, UNITS)), dma((2, COLS, UNITS)),
            dma((2, UNITS)), dma((2, UNITS)),
            dma((2, UNITS)), dma((2, UNITS)),
            dma((2,)), dma((2,)),
            dma((2, 5)), dma((2, 4)),
            dma((2, 5)), dma((2, 4)),
        ],
        compiler_params=pltpu.CompilerParams(
            collective_id=0, has_side_effects=True, vmem_limit_bytes=56 * 2**20
        ),
        name="project_panels",
    )(panel_index, matrix, basis_matrix)


def solution(mesh):
    return jax.shard_map(
        body,
        mesh=mesh,
        in_specs=(P(("grp", "row"), "col"), P(("grp", "row"), "col"), P("grp", None)),
        out_specs=P(("grp", "col", "row"), None),
        check_vma=False,
    )
```

time: 308 us -> 101 us (0.33)
  waiting for transfers between devices: 262 us -> 0 us
  Pallas kernels: 0 us -> 99.2 us
  matrix products: 24 us -> 0 us
  between operations: 15.7 us -> 0.01 us
    psum x2 -> x0, waiting for transfers between devices: 103 us -> none  [the longest x1 53.8 us: body(): columns = lax.psum(masked, 'col')]
    pallas_call x0 -> x1, Pallas kernels: none -> 99.2 us  [body(): pl.pallas_call(kernel, out_shape=jax.ShapeDtypeStruct((piece, 2 * PANEL),...]
    all_gather x1 -> x0, waiting for transfers between devices: 98.2 us -> none  [body(): gathered = lax.all_gather(columns, 'row', axis=0, tiled=True)]
    reduce_scatter x1 -> x0, waiting for transfers between devices: 60.2 us -> none  [body(): lax.psum_scatter(contribution, 'row', scatter_dimension=0, tiled=True)]
    dot_general x2 -> x0, matrix products: 24 us -> none  [the longest x1 16.6 us: body(): jnp.dot(matrix, needed, precision=lax.Precision.HIGHEST, preferred_elemen...]
  transfers between devices with their start and end apart: 4 -> 0, of which waited for: 4 -> 0; matrix products, arithmetic and copies ran while one was open for 0% -> 0% of each run, Pallas kernels for 0% -> 0%
where the time goes in v1:
time: 101 us
  Pallas kernels  99.2 us (98%)
  local copies, waits for them, and re-layouts  1.57 us (2%)
    pallas_call x1, Pallas kernels, body(): pl.pallas_call(kernel, out_shape=jax.ShapeDtypeStruct((piece, 2 * PANEL),...  99.2 us

profile of v1, /device:TPU:16, one launch (start us, length us, event | category | flops | bytes accessed | tf_op | source)
XLA Modules:
  0.0 100.7 jit_solution(10224973107904830522)
XLA Ops:
  0.0 99.2 %project_panels.1 = f32[128,256]{1,0:T(8,128)} custom-call(s32[2,2]{1,0:T(2,128)} %index_ref.1, f32[512,2048]{1,0:T(8,128)} %matrix_hbm.1, f32[512,2048]{1,0:T(8,128)} %basis_hbm.1), custom_call_target="tpu_custom_call" | custom-call | tf_op jit(solution)/shard_map/project_panels/pallas_call | solution.py:321
  99.2 1.6 %copy.5 = f32[128,256]{1,0:T(8,128)} copy(f32[128,256]{1,0:T(8,128)} %project_panels.1) | data formatting | bytes 262144

commit v2 on v0

v2 whole, which is shorter than its diff:
```python
import functools

import jax
import jax.numpy as jnp
from jax import lax
from jax.experimental import pallas as pl
from jax.experimental.pallas import tpu as pltpu
from jax.sharding import PartitionSpec as P

PANEL = 128
MESH = pl.DeviceIdType.MESH
PLANES = 8
COLS = 4
PASSES = 2
UNITS = 4
PARTS = 2
BF16 = jnp.bfloat16
F32 = jnp.float32


def split(value):
    high = value.astype(BF16)
    return high, (value - high.astype(F32)).astype(BF16)


def dot3(a_high, a_low, b_high, b_low):
    total = jnp.dot(a_high, b_high, preferred_element_type=F32)
    total += jnp.dot(a_high, b_low, preferred_element_type=F32)
    total += jnp.dot(a_low, b_high, preferred_element_type=F32)
    return total


def kernel(
    index_ref, matrix_hbm, basis_hbm, out_ref,
    matrix_v, basis_v, m_high, m_low, qt_high, qt_low,
    pair_out, pair_in, ring, chosen, x_high, x_low, y_high, y_low,
    image, image_in, image_sum, image_pair,
    proj, proj_in, proj_sum, far_in, mid_out, mid_in, near_in,
    load_sem, pair_s, pair_r, up_s, up_r, down_s, down_r,
    cross_s, cross_r, twin_s, twin_r, swap_s, swap_r, half_s, half_r,
    mate_s, mate_r, far_s, far_r, mid_s, mid_r, near_s, near_r,
):
    grp = lax.axis_index("grp")
    row = lax.axis_index("row")
    col = lax.axis_index("col")
    plane = row // 2
    core = lax.rem(row, 2)
    half = col // 2
    slot = lax.rem(col, 2)
    rows = basis_v.shape[0]
    cols = basis_v.shape[1]
    piece = cols // (2 * PLANES)
    per_col = cols // PANEL
    carried = rows // 2
    unit = carried // UNITS
    portion = carried // PARTS

    def at(r, c):
        return (grp, r, c)

    def along(step):
        return at(lax.rem(plane + PLANES + step, PLANES) * 2 + core, col)

    twin = at(row + 1 - 2 * core, col)
    above = along(1)
    below = along(-1)
    pair = at(row, col + 1 - 2 * slot)
    mirror = at(row, 3 - col)
    across = at(row, lax.rem(col + 2, COLS))

    load_basis = pltpu.make_async_copy(basis_hbm, basis_v, load_sem.at[0])
    load_matrix = pltpu.make_async_copy(matrix_hbm, matrix_v, load_sem.at[1])
    load_basis.start()

    barrier = pltpu.get_barrier_semaphore()
    partners = (twin, above, below, along(2), along(-2), pair, mirror, across)
    for other in partners:
        pl.semaphore_signal(barrier, inc=1, device_id=other, device_id_type=MESH)

    sends = []

    def send(src, dst, send_sem, recv_sem, target):
        copy = pltpu.make_async_remote_copy(
            src_ref=src, dst_ref=dst, send_sem=send_sem, recv_sem=recv_sem,
            device_id=target, device_id_type=MESH,
        )
        copy.start()
        sends.append(copy)

    def arrived(ref, sem):
        pltpu.make_async_copy(ref, ref, sem).wait()

    load_basis.wait()
    load_matrix.start()
    span_rows = min(64, carried)

    def pick(s, i, row_half):
        index = index_ref[half, s] - slot * per_col
        at_rows = pl.ds(pl.multiple_of(row_half * carried + i * span_rows, span_rows), span_rows)
        index_v = jnp.full((span_rows, PANEL), index, jnp.int32)
        total = jnp.zeros((span_rows, PANEL), F32)
        for j in range(per_col):
            total = jnp.where(index_v == j, basis_v[at_rows, j * PANEL:(j + 1) * PANEL], total)
        return total

    def pick_other(i, carry):
        for s in range(PASSES):
            at_rows = pl.ds(pl.multiple_of(i * span_rows, span_rows), span_rows)
            pair_out[s, at_rows] = pick(s, i, 1 - slot)
        return carry

    def pick_own(i, carry):
        for s in range(PASSES):
            at_rows = pl.ds(pl.multiple_of(i * span_rows, span_rows), span_rows)
            ring[0, s, at_rows] = pick(s, i, slot)
        return carry

    lax.fori_loop(0, carried // span_rows, pick_other, 0)
    pl.semaphore_wait(barrier, len(partners))

    def of_unit(u):
        return pl.ds(u * unit, unit)

    def of_portion(v):
        return pl.ds(v * portion, portion)

    for s in range(PASSES):
        for u in range(UNITS):
            send(
                pair_out.at[s, of_unit(u)], pair_in.at[s, of_unit(u)],
                pair_s.at[s, u], pair_r.at[s, u], pair,
            )
    lax.fori_loop(0, carried // span_rows, pick_own, 0)

    def split_matrix(b):
        at_cols = pl.ds(b * 2 * PANEL, 2 * PANEL)
        m_high[:, at_cols], m_low[:, at_cols] = split(matrix_v[:, at_cols])

    def split_basis(b):
        at_cols = pl.ds(b * PANEL, PANEL)
        qt_high[at_cols, :], qt_low[at_cols, :] = split(basis_v[:, at_cols].T)

    matrix_work = [functools.partial(split_matrix, b) for b in range(cols // (2 * PANEL))]
    basis_work = [functools.partial(split_basis, b) for b in range(cols // PANEL)]

    def do(work, count):
        for _ in range(min(count, len(work))):
            work.pop(0)()

    cross = []

    def deliver(s, d, v):
        source = lax.rem(plane + PLANES - d, PLANES)
        target = source // 2
        odd = lax.rem(source, 2)
        src = ring.at[d, s, of_portion(v)]
        first = pl.multiple_of(slot * carried + v * portion, portion)
        dst = chosen.at[2 * odd + core, 2 * half + s, pl.ds(first, portion)]
        sem = cross_r.at[odd, s, col, v]
        copy = pltpu.make_async_remote_copy(
            src_ref=src, dst_ref=dst, send_sem=cross_s.at[d, s, v], recv_sem=sem,
            device_id=at(row, target), device_id_type=MESH,
        )

        @pl.when(target != col)
        def _():
            copy.start()

        @pl.when(target == col)
        def _():
            pltpu.make_async_copy(src, dst, sem).start()

        cross.append((target, copy))

    def go_up(s, d, u):
        send(
            ring.at[d, s, of_unit(u)], ring.at[d + 1, s, of_unit(u)],
            up_s.at[d, s, u], up_r.at[d, s, u], above,
        )

    def go_down(s, d, u):
        send(
            ring.at[(PLANES - d) % PLANES, s, of_unit(u)],
            ring.at[PLANES - 1 - d, s, of_unit(u)],
            down_s.at[d, s, u], down_r.at[d, s, u], below,
        )

    def handle(s, d):
        for u in range(UNITS):
            up_far, down_far = u % 2 == 0, u % 2 == 1
            if d == 0:
                arrived(pair_in.at[s, of_unit(u)], pair_r.at[s, u])
                ring[0, s, of_unit(u)] = ring[0, s, of_unit(u)] + pair_in[s, of_unit(u)]
                go_up(s, 0, u)
                go_down(s, 0, u)
            if d > 0 and (d < 4 or up_far):
                arrived(ring.at[d, s, of_unit(u)], up_r.at[d - 1, s, u])
                if d < 3 or (d == 3 and up_far):
                    go_up(s, d, u)
            if d > 0 and (d < 4 or down_far):
                arrived(ring.at[PLANES - d, s, of_unit(u)], down_r.at[d - 1, s, u])
                if d < 3 or (d == 3 and down_far):
                    go_down(s, d, u)
            if u % 2 == 1:
                deliver(s, d, u // 2)
                if 0 < d < 4:
                    deliver(s, PLANES - d, u // 2)

    def share(s, odd):
        for v in range(PARTS):
            for c in range(COLS):
                first = (c % 2) * carried + v * portion
                ref = chosen.at[2 * odd + core, 2 * (c // 2) + s, pl.ds(first, portion)]
                arrived(ref, cross_r.at[odd, s, c, v])
                send(ref, ref, twin_s.at[odd, s, c, v], twin_r.at[odd, s, c, v], twin)

    def shared(s, odd):
        for v in range(PARTS):
            for c in range(COLS):
                first = (c % 2) * carried + v * portion
                ref = chosen.at[2 * odd + 1 - core, 2 * (c // 2) + s, pl.ds(first, portion)]
                arrived(ref, twin_r.at[odd, s, c, v])

    def multiply(s, block, first):
        value = jnp.concatenate([chosen[block, s], chosen[block, 2 + s]], axis=1)
        x_high[...], x_low[...] = split(value)
        at_cols = pl.ds(pl.multiple_of(block * rows, rows), rows)

        def body(i, carry):
            at_rows = pl.ds(pl.multiple_of(i * carried, carried), carried)
            term = dot3(m_high[at_rows, at_cols], m_low[at_rows, at_cols], x_high[...], x_low[...])
            for h in range(2):
                piece_h = term[:, h * PANEL:(h + 1) * PANEL]
                image[s, h, at_rows] = piece_h if first else image[s, h, at_rows] + piece_h
            return carry
        lax.fori_loop(0, 2, body, 0)

    def half_rows(v):
        return pl.ds(v * carried, carried)

    def swap(s, v):
        send(
            image.at[s, 1 - half, half_rows(v)], image_in.at[s, half_rows(v)],
            swap_s.at[s, v], swap_r.at[s, v], mirror,
        )

    def add_swap(s, v):
        at_rows = half_rows(v)
        arrived(image_in.at[s, at_rows], swap_r.at[s, v])
        image_sum[s, at_rows] = image[s, half, at_rows] + image_in[s, at_rows]
        send(
            image_sum.at[s, at_rows], image_pair.at[s, at_rows],
            half_s.at[s, v], half_r.at[s, v], pair,
        )

    order = (4, 3, 5, 2, 6, 1, 7, 0)
    groups = ((0, 3), (3, 8))

    def project(s, parity, group):
        for i in range(*groups[group]):
            target = lax.rem(plane + order[i], PLANES)
            at_rows = pl.ds(pl.multiple_of((2 * target + parity) * piece, piece), piece)
            proj[s, parity, i] = dot3(
                qt_high[at_rows, :], qt_low[at_rows, :], y_high[s], y_low[s]
            )

    def begin(s):
        for v in range(2):
            arrived(image_pair.at[s, half_rows(v)], half_r.at[s, v])
        y_high[s], y_low[s] = split(image_sum[s] + image_pair[s])

    def exchange(s, group):
        first, last = groups[group]
        span_i = pl.ds(first, last - first)
        project(s, 1 - core, group)
        send(
            proj.at[s, 1 - core, span_i], proj_in.at[s, span_i],
            mate_s.at[s, group], mate_r.at[s, group], twin,
        )
        project(s, core, group)

    def combine(s, group):
        first, last = groups[group]
        span_i = pl.ds(first, last - first)
        arrived(proj_in.at[s, span_i], mate_r.at[s, group])
        proj_sum[s, span_i] = proj[s, core, span_i] + proj_in[s, span_i]

    near_rows = piece // 2

    def whole(sign):
        return pl.ds(0, near_rows) if sign == 0 else pl.ds(near_rows, near_rows)

    def place(sign, d):
        return order.index(d if sign == 0 else PLANES - d)

    def toward(sign, d):
        return along(d if sign == 0 else -d)

    def sum_far(s):
        for sign in range(2):
            send(
                proj_sum.at[s, place(sign, 4), whole(sign)], far_in.at[s, sign, 1, whole(sign)],
                far_s.at[s, sign, 1], far_r.at[s, sign, 1], toward(sign, 2),
            )
            send(
                proj_sum.at[s, place(sign, 3)], far_in.at[s, sign, 0],
                far_s.at[s, sign, 0], far_r.at[s, sign, 0], toward(sign, 1),
            )

    def sum_near(s):
        for sign in range(2):
            send(
                proj_sum.at[s, place(sign, 1)], near_in.at[s, sign],
                near_s.at[s, sign], near_r.at[s, sign], toward(sign, 1),
            )

    def sum_mid(s):
        for sign in range(2):
            arrived(far_in.at[s, sign, 1, whole(sign)], far_r.at[s, sign, 1])
            arrived(far_in.at[s, sign, 0], far_r.at[s, sign, 0])
            mid_out[s, sign] = proj_sum[s, place(sign, 2)] + far_in[s, sign, 0]
            mid_out[s, sign, whole(sign)] = mid_out[s, sign, whole(sign)] + far_in[s, sign, 1, whole(sign)]
            send(
                mid_out.at[s, sign], mid_in.at[s, sign],
                mid_s.at[s, sign], mid_r.at[s, sign], toward(sign, 2),
            )

    def finish(s):
        total = proj_sum[s, order.index(0)]
        for sign in range(2):
            arrived(near_in.at[s, sign], near_r.at[s, sign])
            arrived(mid_in.at[s, sign], mid_r.at[s, sign])
            total = total + near_in[s, sign] + mid_in[s, sign]
        out_ref[:, s * PANEL:(s + 1) * PANEL] = total

    handle(0, 0)
    load_matrix.wait()
    do(matrix_work, 1)
    handle(0, 1)
    do(matrix_work, 2)
    handle(0, 2)
    do(matrix_work, 2)
    handle(0, 3)
    handle(1, 0)
    do(matrix_work, 2)
    handle(0, 4)
    do(matrix_work, 1)
    handle(1, 1)
    do(basis_work, 2)
    handle(1, 2)
    do(basis_work, 2)
    handle(1, 3)
    share(0, 0)
    share(0, 1)
    handle(1, 4)
    multiply(0, core, True)
    multiply(0, 2 + core, False)
    shared(0, 0)
    multiply(0, 1 - core, False)
    shared(0, 1)
    multiply(0, 3 - core, False)
    swap(0, 0)
    swap(0, 1)
    do(basis_work, 4)
    share(1, 0)
    share(1, 1)
    multiply(1, core, True)
    multiply(1, 2 + core, False)
    shared(1, 0)
    multiply(1, 1 - core, False)
    shared(1, 1)
    multiply(1, 3 - core, False)
    swap(1, 0)
    swap(1, 1)
    add_swap(0, 0)
    add_swap(0, 1)
    do(basis_work, len(basis_work))
    begin(0)
    exchange(0, 0)
    combine(0, 0)
    sum_far(0)
    add_swap(1, 0)
    exchange(0, 1)
    combine(0, 1)
    add_swap(1, 1)
    sum_mid(0)
    sum_near(0)
    begin(1)
    exchange(1, 0)
    combine(1, 0)
    sum_far(1)
    exchange(1, 1)
    combine(1, 1)
    sum_mid(1)
    sum_near(1)
    finish(0)
    finish(1)

    for copy in sends:
        copy.wait_send()
    for target, copy in cross:
        @pl.when(target != col)
        def _(copy=copy):
            copy.wait_send()


def body(matrix, basis_matrix, panel_index):
    rows, cols = matrix.shape
    piece = cols // (2 * PLANES)
    carried = rows // 2
    vmem = pltpu.VMEM

    def pairs(*shape):
        return [pltpu.SemaphoreType.DMA(shape), pltpu.SemaphoreType.DMA(shape)]

    return pl.pallas_call(
        kernel,
        out_shape=jax.ShapeDtypeStruct((piece, 2 * PANEL), F32),
        in_specs=[
            pl.BlockSpec(memory_space=pltpu.SMEM),
            pl.BlockSpec(memory_space=pl.ANY),
            pl.BlockSpec(memory_space=pl.ANY),
        ],
        out_specs=pl.BlockSpec(memory_space=pltpu.VMEM),
        scratch_shapes=[
            vmem((rows, cols), F32),
            vmem((rows, cols), F32),
            vmem((rows, cols), BF16),
            vmem((rows, cols), BF16),
            vmem((cols, rows), BF16),
            vmem((cols, rows), BF16),
            vmem((PASSES, carried, PANEL), F32),
            vmem((PASSES, carried, PANEL), F32),
            vmem((PLANES, PASSES, carried, PANEL), F32),
            vmem((4, COLS, rows, PANEL), F32),
            vmem((rows, 2 * PANEL), BF16),
            vmem((rows, 2 * PANEL), BF16),
            vmem((PASSES, rows, PANEL), BF16),
            vmem((PASSES, rows, PANEL), BF16),
            vmem((PASSES, 2, rows, PANEL), F32),
            vmem((PASSES, rows, PANEL), F32),
            vmem((PASSES, rows, PANEL), F32),
            vmem((PASSES, rows, PANEL), F32),
            vmem((PASSES, 2, PLANES, piece, PANEL), F32),
            vmem((PASSES, PLANES, piece, PANEL), F32),
            vmem((PASSES, PLANES, piece, PANEL), F32),
            vmem((PASSES, 2, 2, piece, PANEL), F32),
            vmem((PASSES, 2, piece, PANEL), F32),
            vmem((PASSES, 2, piece, PANEL), F32),
            vmem((PASSES, 2, piece, PANEL), F32),
            pltpu.SemaphoreType.DMA((2,)),
            *pairs(PASSES, UNITS),
            *pairs(4, PASSES, UNITS),
            *pairs(4, PASSES, UNITS),
            pltpu.SemaphoreType.DMA((PLANES, PASSES, PARTS)),
            pltpu.SemaphoreType.DMA((2, PASSES, COLS, PARTS)),
            *pairs(2, PASSES, COLS, PARTS),
            *pairs(PASSES, 2),
            *pairs(PASSES, 2),
            *pairs(PASSES, 2),
            *pairs(PASSES, 2, 2),
            *pairs(PASSES, 2),
            *pairs(PASSES, 2),
        ],
        compiler_params=pltpu.CompilerParams(
            collective_id=0, has_side_effects=True, vmem_limit_bytes=56 * 2**20
        ),
        name="project_panels",
    )(panel_index, matrix, basis_matrix)


def solution(mesh):
    return jax.shard_map(
        body,
        mesh=mesh,
        in_specs=(P(("grp", "row"), "col"), P(("grp", "row"), "col"), P("grp", None)),
        out_specs=P(("grp", "col", "row"), None),
        check_vma=False,
    )
```

time: 308 us -> 83.6 us (0.27)
  waiting for transfers between devices: 262 us -> 0 us
  Pallas kernels: 0 us -> 81.1 us
  matrix products: 24 us -> 0 us
  between operations: 15.7 us -> 0.01 us
    psum x2 -> x0, waiting for transfers between devices: 103 us -> none  [the longest x1 53.8 us: body(): columns = lax.psum(masked, 'col')]
    all_gather x1 -> x0, waiting for transfers between devices: 98.2 us -> none  [body(): gathered = lax.all_gather(columns, 'row', axis=0, tiled=True)]
    pallas_call x0 -> x1, Pallas kernels: none -> 81.1 us  [body(): pl.pallas_call(kernel, out_shape=jax.ShapeDtypeStruct((piece, 2 * PANEL),...]
    reduce_scatter x1 -> x0, waiting for transfers between devices: 60.2 us -> none  [body(): lax.psum_scatter(contribution, 'row', scatter_dimension=0, tiled=True)]
    dot_general x2 -> x0, matrix products: 24 us -> none  [the longest x1 16.6 us: body(): jnp.dot(matrix, needed, precision=lax.Precision.HIGHEST, preferred_elemen...]
  transfers between devices with their start and end apart: 4 -> 0, of which waited for: 4 -> 0; matrix products, arithmetic and copies ran while one was open for 0% -> 0% of each run, Pallas kernels for 0% -> 0%
where the time goes in v2:
time: 83.6 us; the launch traced here: 82.7 us
  Pallas kernels  81.1 us (97%)
  local copies, waits for them, and re-layouts  1.57 us (2%)
    pallas_call x1, Pallas kernels, body(): pl.pallas_call(kernel, out_shape=jax.ShapeDtypeStruct((piece, 2 * PANEL),...  81.1 us

profile of v2, /device:TPU:16, one launch (start us, length us, event | category | flops | bytes accessed | tf_op | source)
XLA Modules:
  0.0 82.7 jit_solution(5608594363940490233)
XLA Ops:
  0.0 81.1 %project_panels.1 = f32[128,256]{1,0:T(8,128)} custom-call(s32[2,2]{1,0:T(2,128)} %index_ref.1, f32[512,2048]{1,0:T(8,128)} %matrix_hbm.1, f32[512,2048]{1,0:T(8,128)} %basis_hbm.1), custom_call_target="tpu_custom_call" | custom-call | tf_op jit(solution)/shard_map/project_panels/pallas_call | solution.py:416
  81.1 1.6 %copy.5 = f32[128,256]{1,0:T(8,128)} copy(f32[128,256]{1,0:T(8,128)} %project_panels.1) | data formatting | bytes 262144

commit v3 on v2

--- a/solution.py
+++ b/solution.py
@@ -14,6 +14,7 @@
 PASSES = 2
 UNITS = 4
 PARTS = 2
+SWAPS = 4
 BF16 = jnp.bfloat16
 F32 = jnp.float32
 
@@ -236,7 +237,7 @@
         lax.fori_loop(0, 2, body, 0)
 
     def half_rows(v):
-        return pl.ds(v * carried, carried)
+        return pl.ds(v * (rows // SWAPS), rows // SWAPS)
 
     def swap(s, v):
         send(
@@ -265,7 +266,7 @@
             )
 
     def begin(s):
-        for v in range(2):
+        for v in range(SWAPS):
             arrived(image_pair.at[s, half_rows(v)], half_r.at[s, v])
         y_high[s], y_low[s] = split(image_sum[s] + image_pair[s])
 
@@ -335,24 +336,27 @@
 
     handle(0, 0)
     load_matrix.wait()
-    do(matrix_work, 1)
+    do(matrix_work, 2)
     handle(0, 1)
     do(matrix_work, 2)
     handle(0, 2)
     do(matrix_work, 2)
-    handle(0, 3)
     handle(1, 0)
     do(matrix_work, 2)
+    handle(0, 3)
+    do(basis_work, 0)
+    handle(1, 1)
+    do(basis_work, 0)
     handle(0, 4)
-    do(matrix_work, 1)
-    handle(1, 1)
-    do(basis_work, 2)
+    do(basis_work, 0)
     handle(1, 2)
-    do(basis_work, 2)
+    do(basis_work, 0)
     handle(1, 3)
+    do(basis_work, 0)
+    handle(1, 4)
+    do(basis_work, 0)
     share(0, 0)
     share(0, 1)
-    handle(1, 4)
     multiply(0, core, True)
     multiply(0, 2 + core, False)
     shared(0, 0)
@@ -361,41 +365,47 @@
     multiply(0, 3 - core, False)
     swap(0, 0)
     swap(0, 1)
-    do(basis_work, 4)
+    swap(0, 2)
+    swap(0, 3)
     share(1, 0)
     share(1, 1)
     multiply(1, core, True)
     multiply(1, 2 + core, False)
+    add_swap(0, 0)
+    add_swap(0, 1)
+    add_swap(0, 2)
+    add_swap(0, 3)
     shared(1, 0)
     multiply(1, 1 - core, False)
     shared(1, 1)
     multiply(1, 3 - core, False)
     swap(1, 0)
     swap(1, 1)
-    add_swap(0, 0)
-    add_swap(0, 1)
-    do(basis_work, len(basis_work))
+    swap(1, 2)
+    swap(1, 3)
+    do(basis_work, 16)
     begin(0)
     exchange(0, 0)
     combine(0, 0)
     sum_far(0)
     add_swap(1, 0)
+    add_swap(1, 1)
     exchange(0, 1)
+    add_swap(1, 2)
+    add_swap(1, 3)
     combine(0, 1)
-    add_swap(1, 1)
+    sum_near(0)
     sum_mid(0)
-    sum_near(0)
     begin(1)
     exchange(1, 0)
     combine(1, 0)
     sum_far(1)
     exchange(1, 1)
     combine(1, 1)
+    sum_near(1)
     sum_mid(1)
-    sum_near(1)
     finish(0)
     finish(1)
-
     for copy in sends:
         copy.wait_send()
     for target, copy in cross:
@@ -455,8 +465,8 @@
             pltpu.SemaphoreType.DMA((PLANES, PASSES, PARTS)),
             pltpu.SemaphoreType.DMA((2, PASSES, COLS, PARTS)),
             *pairs(2, PASSES, COLS, PARTS),
-            *pairs(PASSES, 2),
-            *pairs(PASSES, 2),
+            *pairs(PASSES, SWAPS),
+            *pairs(PASSES, SWAPS),
             *pairs(PASSES, 2),
             *pairs(PASSES, 2, 2),
             *pairs(PASSES, 2),

time: 83.6 us -> 80.6 us (0.964)
  Pallas kernels: 81.1 us -> 78.9 us
    pallas_call x1, Pallas kernels: 81.1 us -> 78.9 us  [body(): pl.pallas_call(kernel, out_shape=jax.ShapeDtypeStruct((piece, 2 * PANEL),...]
where the time goes in v3:
time: 80.6 us; the launch traced here: 80.4 us
  Pallas kernels  78.9 us (98%)
  local copies, waits for them, and re-layouts  1.57 us (2%)
    pallas_call x1, Pallas kernels, body(): pl.pallas_call(kernel, out_shape=jax.ShapeDtypeStruct((piece, 2 * PANEL),...  78.9 us

profile of v3, /device:TPU:16, one launch (start us, length us, event | category | flops | bytes accessed | tf_op | source)
XLA Modules:
  0.0 80.4 jit_solution(9547511474047122755)
XLA Ops:
  0.0 78.9 %project_panels.1 = f32[128,256]{1,0:T(8,128)} custom-call(s32[2,2]{1,0:T(2,128)} %index_ref.1, f32[512,2048]{1,0:T(8,128)} %matrix_hbm.1, f32[512,2048]{1,0:T(8,128)} %basis_hbm.1), custom_call_target="tpu_custom_call" | custom-call | tf_op jit(solution)/shard_map/project_panels/pallas_call | solution.py:426
  78.9 1.6 %copy.5 = f32[128,256]{1,0:T(8,128)} copy(f32[128,256]{1,0:T(8,128)} %project_panels.1) | data formatting | bytes 262144

commit v4 on v3

--- a/solution.py
+++ b/solution.py
@@ -69,9 +69,17 @@
     mirror = at(row, 3 - col)
     across = at(row, lax.rem(col + 2, COLS))
 
-    load_basis = pltpu.make_async_copy(basis_hbm, basis_v, load_sem.at[0])
+    def load_half(which, row_half):
+        at_rows = pl.ds(pl.multiple_of(row_half * carried, carried), carried)
+        return pltpu.make_async_copy(
+            basis_hbm.at[at_rows], basis_v.at[at_rows], load_sem.at[which]
+        )
+
+    load_other = load_half(0, 1 - slot)
+    load_own = load_half(2, slot)
     load_matrix = pltpu.make_async_copy(matrix_hbm, matrix_v, load_sem.at[1])
-    load_basis.start()
+    load_other.start()
+    load_own.start()
 
     barrier = pltpu.get_barrier_semaphore()
     partners = (twin, above, below, along(2), along(-2), pair, mirror, across)
@@ -91,8 +99,7 @@
     def arrived(ref, sem):
         pltpu.make_async_copy(ref, ref, sem).wait()
 
-    load_basis.wait()
-    load_matrix.start()
+    load_other.wait()
     span_rows = min(64, carried)
 
     def pick(s, i, row_half):
@@ -104,19 +111,14 @@
             total = jnp.where(index_v == j, basis_v[at_rows, j * PANEL:(j + 1) * PANEL], total)
         return total
 
-    def pick_other(i, carry):
-        for s in range(PASSES):
+    def pick_into(ref, s, row_half):
+        def body(i, carry):
             at_rows = pl.ds(pl.multiple_of(i * span_rows, span_rows), span_rows)
-            pair_out[s, at_rows] = pick(s, i, 1 - slot)
-        return carry
-
-    def pick_own(i, carry):
-        for s in range(PASSES):
-            at_rows = pl.ds(pl.multiple_of(i * span_rows, span_rows), span_rows)
-            ring[0, s, at_rows] = pick(s, i, slot)
-        return carry
-
-    lax.fori_loop(0, carried // span_rows, pick_other, 0)
+            ref[s, at_rows] = pick(s, i, row_half)
+            return carry
+        lax.fori_loop(0, carried // span_rows, body, 0)
+
+    pick_into(pair_out, 0, 1 - slot)
     pl.semaphore_wait(barrier, len(partners))
 
     def of_unit(u):
@@ -125,13 +127,19 @@
     def of_portion(v):
         return pl.ds(v * portion, portion)
 
-    for s in range(PASSES):
+    def exchange_pair(s):
         for u in range(UNITS):
             send(
                 pair_out.at[s, of_unit(u)], pair_in.at[s, of_unit(u)],
                 pair_s.at[s, u], pair_r.at[s, u], pair,
             )
-    lax.fori_loop(0, carried // span_rows, pick_own, 0)
+
+    exchange_pair(0)
+    load_own.wait()
+    load_matrix.start()
+    pick_into(ring.at[0], 0, slot)
+    pick_into(pair_out, 1, 1 - slot)
+    pick_into(ring.at[0], 1, slot)
 
     def split_matrix(b):
         at_cols = pl.ds(b * 2 * PANEL, 2 * PANEL)
@@ -335,6 +343,7 @@
         out_ref[:, s * PANEL:(s + 1) * PANEL] = total
 
     handle(0, 0)
+    exchange_pair(1)
     load_matrix.wait()
     do(matrix_work, 2)
     handle(0, 1)
@@ -458,7 +467,7 @@
             vmem((PASSES, 2, piece, PANEL), F32),
             vmem((PASSES, 2, piece, PANEL), F32),
             vmem((PASSES, 2, piece, PANEL), F32),
-            pltpu.SemaphoreType.DMA((2,)),
+            pltpu.SemaphoreType.DMA((3,)),
             *pairs(PASSES, UNITS),
             *pairs(4, PASSES, UNITS),
             *pairs(4, PASSES, UNITS),

time: 80.6 us -> 80.5 us (level)
  no operation moved by 1% of the time
where the time goes in v4:
time: 80.5 us; the launch traced here: 80.1 us
  Pallas kernels  78.5 us (98%)
  local copies, waits for them, and re-layouts  1.57 us (2%)
    pallas_call x1, Pallas kernels, body(): pl.pallas_call(kernel, out_shape=jax.ShapeDtypeStruct((piece, 2 * PANEL),...  78.5 us

profile of v4, /device:TPU:16, one launch (start us, length us, event | category | flops | bytes accessed | tf_op | source)
XLA Modules:
  0.0 80.1 jit_solution(6523843426194881215)
XLA Ops:
  0.0 78.5 %project_panels.1 = f32[128,256]{1,0:T(8,128)} custom-call(s32[2,2]{1,0:T(2,128)} %index_ref.1, f32[512,2048]{1,0:T(8,128)} %matrix_hbm.1, f32[512,2048]{1,0:T(8,128)} %basis_hbm.1), custom_call_target="tpu_custom_call" | custom-call | tf_op jit(solution)/shard_map/project_panels/pallas_call | solution.py:435
  78.6 1.6 %copy.5 = f32[128,256]{1,0:T(8,128)} copy(f32[128,256]{1,0:T(8,128)} %project_panels.1) | data formatting | bytes 262144

commit v5 on v3

--- a/solution.py
+++ b/solution.py
@@ -33,7 +33,7 @@
 
 def kernel(
     index_ref, matrix_hbm, basis_hbm, out_ref,
-    matrix_v, basis_v, m_high, m_low, qt_high, qt_low,
+    matrix_v, basis_v, m_high, m_low, q_high, q_low,
     pair_out, pair_in, ring, chosen, x_high, x_low, y_high, y_low,
     image, image_in, image_sum, image_pair,
     proj, proj_in, proj_sum, far_in, mid_out, mid_in, near_in,
@@ -138,11 +138,11 @@
         m_high[:, at_cols], m_low[:, at_cols] = split(matrix_v[:, at_cols])
 
     def split_basis(b):
-        at_cols = pl.ds(b * PANEL, PANEL)
-        qt_high[at_cols, :], qt_low[at_cols, :] = split(basis_v[:, at_cols].T)
+        at_cols = pl.ds(b * 2 * PANEL, 2 * PANEL)
+        q_high[:, at_cols], q_low[:, at_cols] = split(basis_v[:, at_cols])
 
     matrix_work = [functools.partial(split_matrix, b) for b in range(cols // (2 * PANEL))]
-    basis_work = [functools.partial(split_basis, b) for b in range(cols // PANEL)]
+    basis_work = [functools.partial(split_basis, b) for b in range(cols // (2 * PANEL))]
 
     def do(work, count):
         for _ in range(min(count, len(work))):
@@ -222,19 +222,25 @@
                 ref = chosen.at[2 * odd + 1 - core, 2 * (c // 2) + s, pl.ds(first, portion)]
                 arrived(ref, twin_r.at[odd, s, c, v])
 
-    def multiply(s, block, first):
+    def multiply(s, block, first, rest=None):
         value = jnp.concatenate([chosen[block, s], chosen[block, 2 + s]], axis=1)
         x_high[...], x_low[...] = split(value)
         at_cols = pl.ds(pl.multiple_of(block * rows, rows), rows)
 
         def body(i, carry):
-            at_rows = pl.ds(pl.multiple_of(i * carried, carried), carried)
+            at_rows = pl.ds(i * carried if rest else pl.multiple_of(i * carried, carried), carried)
             term = dot3(m_high[at_rows, at_cols], m_low[at_rows, at_cols], x_high[...], x_low[...])
             for h in range(2):
                 piece_h = term[:, h * PANEL:(h + 1) * PANEL]
                 image[s, h, at_rows] = piece_h if first else image[s, h, at_rows] + piece_h
             return carry
-        lax.fori_loop(0, 2, body, 0)
+        if rest is None:
+            lax.fori_loop(0, 2, body, 0)
+        else:
+            for i in range(2):
+                body(i, 0)
+                for v in range(i * SWAPS // 2, (i + 1) * SWAPS // 2):
+                    rest(s, v)
 
     def half_rows(v):
         return pl.ds(v * (rows // SWAPS), rows // SWAPS)
@@ -260,15 +266,15 @@
     def project(s, parity, group):
         for i in range(*groups[group]):
             target = lax.rem(plane + order[i], PLANES)
-            at_rows = pl.ds(pl.multiple_of((2 * target + parity) * piece, piece), piece)
+            at_cols = pl.ds(pl.multiple_of((2 * target + parity) * piece, piece), piece)
             proj[s, parity, i] = dot3(
-                qt_high[at_rows, :], qt_low[at_rows, :], y_high[s], y_low[s]
+                y_high[s], y_low[s], q_high[:, at_cols], q_low[:, at_cols]
             )
 
     def begin(s):
         for v in range(SWAPS):
             arrived(image_pair.at[s, half_rows(v)], half_r.at[s, v])
-        y_high[s], y_low[s] = split(image_sum[s] + image_pair[s])
+        y_high[s], y_low[s] = split((image_sum[s] + image_pair[s]).T)
 
     def exchange(s, group):
         first, last = groups[group]
@@ -332,7 +338,7 @@
             arrived(near_in.at[s, sign], near_r.at[s, sign])
             arrived(mid_in.at[s, sign], mid_r.at[s, sign])
             total = total + near_in[s, sign] + mid_in[s, sign]
-        out_ref[:, s * PANEL:(s + 1) * PANEL] = total
+        out_ref[:, s * PANEL:(s + 1) * PANEL] = total.T
 
     handle(0, 0)
     load_matrix.wait()
@@ -362,11 +368,7 @@
     shared(0, 0)
     multiply(0, 1 - core, False)
     shared(0, 1)
-    multiply(0, 3 - core, False)
-    swap(0, 0)
-    swap(0, 1)
-    swap(0, 2)
-    swap(0, 3)
+    multiply(0, 3 - core, False, swap)
     share(1, 0)
     share(1, 1)
     multiply(1, core, True)
@@ -378,11 +380,7 @@
     shared(1, 0)
     multiply(1, 1 - core, False)
     shared(1, 1)
-    multiply(1, 3 - core, False)
-    swap(1, 0)
-    swap(1, 1)
-    swap(1, 2)
-    swap(1, 3)
+    multiply(1, 3 - core, False, swap)
     do(basis_work, 16)
     begin(0)
     exchange(0, 0)
@@ -437,16 +435,16 @@
             vmem((rows, cols), F32),
             vmem((rows, cols), BF16),
             vmem((rows, cols), BF16),
-            vmem((cols, rows), BF16),
-            vmem((cols, rows), BF16),
+            vmem((rows, cols), BF16),
+            vmem((rows, cols), BF16),
             vmem((PASSES, carried, PANEL), F32),
             vmem((PASSES, carried, PANEL), F32),
             vmem((PLANES, PASSES, carried, PANEL), F32),
             vmem((4, COLS, rows, PANEL), F32),
             vmem((rows, 2 * PANEL), BF16),
             vmem((rows, 2 * PANEL), BF16),
-            vmem((PASSES, rows, PANEL), BF16),
-            vmem((PASSES, rows, PANEL), BF16),
+            vmem((PASSES, PANEL, rows), BF16),
+            vmem((PASSES, PANEL, rows), BF16),
             vmem((PASSES, 2, rows, PANEL), F32),
             vmem((PASSES, rows, PANEL), F32),
             vmem((PASSES, rows, PANEL), F32),

time: 80.6 us -> 81.1 us (level)
  no operation moved by 1% of the time
where the time goes in v5:
time: 81.1 us; the launch traced here: 80.9 us
  Pallas kernels  79.3 us (98%)
  local copies, waits for them, and re-layouts  1.57 us (2%)
    pallas_call x1, Pallas kernels, body(): pl.pallas_call(kernel, out_shape=jax.ShapeDtypeStruct((piece, 2 * PANEL),...  79.3 us

profile of v5, /device:TPU:16, one launch (start us, length us, event | category | flops | bytes accessed | tf_op | source)
XLA Modules:
  0.0 80.9 jit_solution(7500119237175755664)
XLA Ops:
  0.0 79.3 %project_panels.1 = f32[128,256]{1,0:T(8,128)} custom-call(s32[2,2]{1,0:T(2,128)} %index_ref.1, f32[512,2048]{1,0:T(8,128)} %matrix_hbm.1, f32[512,2048]{1,0:T(8,128)} %basis_hbm.1), custom_call_target="tpu_custom_call" | custom-call | tf_op jit(solution)/shard_map/project_panels/pallas_call | solution.py:424
  79.3 1.6 %copy.5 = f32[128,256]{1,0:T(8,128)} copy(f32[128,256]{1,0:T(8,128)} %project_panels.1) | data formatting | bytes 262144
